TPU v7x, 32 devices: a whole 2x2x4 slice. The times are simulated.
32 devices in a mesh: sec: 8 (over y, x, core), tile: 4 (over z).
Axes of the slice: x: 2, y: 2, z: 4, core: 2. Of those that a mesh axis runs over, the one named last changes fastest.
Arguments:
- features: bfloat16 [24, 32, 64, 128], P('sec', None, 'tile'), may hold values from -6 to 6
- vote_grad: float32 [24, 2, 64, 128], P('sec', None, 'tile'), may hold values from -6 to 6
- sharpness: float32 [24], P('sec')
- valid_rows: int32 [24], P('sec'), may hold values from 32 to 64
- first_kernel: bfloat16 [3, 3, 64, 64], replicated, may hold values from -0.25 to 0.25
- first_bias: float32 [64], replicated, may hold values from -3 to 3
- second_kernel: bfloat16 [3, 3, 2, 64], replicated, may hold values from -0.25 to 0.25
- second_bias: float32 [2], replicated, may hold values from -3 to 3
Outputs:
- voted_field: float32 [24, 2, 64, 128], P('sec', None, 'tile')
- feature_grad: float32 [24, 32, 64, 128], P('sec', None, 'tile')
All inputs are finite; a program needn't handle non-finite values.
Results may differ from a plain program's by a relative error of at most 0.03.
Values may be sent and summed in bfloat16 or wider, within the bound.
A program may use at most 128 MiB of HBM per device.

v0:
```python
import functools

import jax
import jax.numpy as jnp
from jax import lax
from jax.experimental import pallas as pl
from jax.experimental.pallas import tpu as pltpu
from jax.sharding import PartitionSpec as P

LAGS = 3
BF = jnp.bfloat16
F32 = jnp.float32


def shifted(value, step):
    lanes = value.shape[-1]
    lane = lax.broadcasted_iota(jnp.int32, value.shape, value.ndim - 1)
    rolled = pltpu.roll(value, step % lanes, value.ndim - 1)
    return jnp.where(lane == (0 if step == 1 else lanes - 1), 0.0, rolled)


def compute_kernel(
    prev, own, top, bot, cot, sharp, valid, w1, w1t, b1, w2, w2t, b2,
    voted, grad,
    xs, ab, hid, tap, fld, dfl, dst, dhid, gst, mix,
):
    count, rows, chans, cols = own.shape
    hrows, xrows = rows + 2, rows + 4
    width = b1.shape[0]
    tile = lax.axis_index("tile")
    last = lax.axis_size("tile") - 1

    def lane(row, num=1):
        return slice(row * cols, (row + num) * cols)

    def place(section, row, value):
        wide = value.astype(F32)
        xs[section, 0:chans, lane(row)] = shifted(wide, 1).astype(BF)
        xs[section, chans:2 * chans, lane(row)] = value
        xs[section, 2 * chans:3 * chans, lane(row)] = shifted(wide, -1).astype(BF)

    def place_section(s, _):
        for r in range(rows):
            place(s, r + 2, prev[s, r])
            place(s + count, r + 2, own[s, r])
        return 0

    lax.fori_loop(0, count, place_section, 0)

    def place_halo(s, _):
        for r in range(2):
            place(s, r, top[s, r])
            place(s, rows + 2 + r, bot[s, r])
        return 0

    lax.fori_loop(0, 2 * count, place_halo, 0)

    def first(s, _):
        for r in range(0, hrows, 2):
            stack = jnp.concatenate([xs[s, :, lane(r + dy, 2)] for dy in range(3)], axis=0)
            ab[s, :, lane(r, 2)] = jnp.dot(w1[...], stack, preferred_element_type=F32)
        return 0

    lax.fori_loop(0, 2 * count, first, 0)

    dfl[...] = jnp.zeros_like(dfl)

    def section(s, _):
        for k in range(LAGS):
            for r in range(hrows):
                total = ab[s + count, 0:width, lane(r)] + ab[s + count - 1 - k, width:, lane(r)]
                hid[k * width:(k + 1) * width, lane(r)] = jnp.maximum(total + b1[...], 0.0).astype(BF)

        @pl.when(tile == 0)
        def _():
            hid[:, lane(0)] = jnp.zeros((LAGS * width, cols), BF)

        @pl.when(tile == last)
        def _():
            hid[:, lane(hrows - 1)] = jnp.zeros((LAGS * width, cols), BF)

        tap[...] = jnp.dot(w2[...], hid[...], preferred_element_type=F32)
        for r in range(rows):
            parts = []
            for dx in range(3):
                at = [(dx * 3 + dy) * 8 for dy in range(3)]
                parts.append(sum(tap[at[dy]:at[dy] + 8, lane(r + dy)] for dy in range(3)))
            fld[r] = parts[1] + shifted(parts[0], 1) + shifted(parts[2], -1)

        f = [[fld[:, 2 * k + c, :] + b2[c] for c in range(2)] for k in range(LAGS)]
        dist = {}
        for k in range(LAGS):
            for j in range(k):
                dist[k, j] = dist[j, k] = sum((f[k][c] - f[j][c]) ** 2 for c in range(2))
        logits = [-sharp[s] * sum(dist[k, j] for j in range(LAGS) if j != k) for k in range(LAGS)]
        peak = jnp.maximum(jnp.maximum(logits[0], logits[1]), logits[2])
        expo = [jnp.exp(v - peak) for v in logits]
        norm = expo[0] + expo[1] + expo[2]
        weight = [e / norm for e in expo]
        row = lax.broadcasted_iota(jnp.int32, (rows, cols), 0) + tile * rows
        live = row < valid[s]
        g = [jnp.where(live, cot[s, c], 0.0) for c in range(2)]
        for c in range(2):
            voted[s, c] = sum(weight[k] * f[k][c] for k in range(LAGS))
        dw = [g[0] * f[k][0] + g[1] * f[k][1] for k in range(LAGS)]
        mean = sum(weight[k] * dw[k] for k in range(LAGS))
        q = [-sharp[s] * weight[k] * (dw[k] - mean) for k in range(LAGS)]
        for k in range(LAGS):
            for c in range(2):
                pulled = sum((q[k] + q[j]) * (f[k][c] - f[j][c]) for j in range(LAGS) if j != k)
                dfl[2:2 + rows, 2 * k + c, :] = weight[k] * g[c] + 2.0 * pulled

        zero = jnp.zeros((8, cols), F32)
        moved = [[shifted(dfl[r], -1), dfl[r], shifted(dfl[r], 1)] for r in range(xrows)]
        for r in range(hrows):
            taps = [moved[r - dy + 2][dx] for dx in range(3) for dy in range(3)]
            dst[:, lane(r)] = jnp.concatenate(taps + [zero], axis=0).astype(BF)
        for r in range(0, hrows, 2):
            back = jnp.dot(w2t[...], dst[:, lane(r, 2)], preferred_element_type=F32)
            dhid[s, :, lane(r, 2)] = jnp.where(hid[:, lane(r, 2)].astype(F32) > 0.0, back, 0.0)
        return 0

    lax.fori_loop(0, count, section, 0)

    for t in range(2 * count):
        pairs = [(t + k - count, k - 1) for k in range(1, LAGS + 1) if 0 <= t + k - count < count]
        halves = []
        if t >= count:
            halves.append((0, [(t - count, k) for k in range(LAGS)]))
        if pairs:
            halves.append((width, pairs))
        for r in range(0, hrows, 2):
            for at, terms in halves:
                total = sum(dhid[s, k * width:(k + 1) * width, lane(r, 2)] for s, k in terms)
                gst[at:at + width, lane(r, 2)] = total.astype(BF)
        low = halves[0][0]
        high = halves[-1][0] + width
        for r in range(0, hrows, 2):
            mix[:, lane(r, 2)] = jnp.dot(w1t[:, low:high], gst[low:high, lane(r, 2)], preferred_element_type=F32)
        for x in range(xrows):
            parts = []
            for dx in range(3):
                terms = []
                for dy in range(3):
                    if 0 <= x - dy < hrows:
                        at = (dx * 3 + dy) * chans
                        terms.append(mix[at:at + chans, lane(x - dy)])
                parts.append(sum(terms))
            grad[t, x] = parts[1] + shifted(parts[0], -1) + shifted(parts[2], 1)


def weights_of(first_kernel, first_bias, second_kernel):
    width, chans = first_kernel.shape[2], first_kernel.shape[3] // 2
    split = first_kernel.reshape(3, 3, width, 2, chans)
    w1 = split.transpose(3, 2, 0, 1, 4).reshape(2 * width, 9 * chans)
    w1t = split.transpose(1, 0, 4, 3, 2).reshape(9 * chans, 2 * width)
    taps = second_kernel.transpose(1, 0, 2, 3).reshape(9, 1, 2, 1, width)
    eye = jnp.eye(LAGS, dtype=BF).reshape(1, LAGS, 1, LAGS, 1)
    w2 = (taps * eye).reshape(9, 2 * LAGS, LAGS * width)
    w2 = jnp.pad(w2, ((0, 1), (0, 8 - 2 * LAGS), (0, 0))).reshape(80, LAGS * width)
    b1 = jnp.broadcast_to(first_bias[:, None], (width, 128))
    return w1, w1t, b1, w2, w2.T


def body(
    features, vote_grad, sharpness, valid_rows, first_kernel, first_bias, second_kernel, second_bias
):
    count, chans, rows, cols = features.shape
    secs, tiles = lax.axis_size("sec"), lax.axis_size("tile")
    width = first_kernel.shape[2]
    hrows, xrows = rows + 2, rows + 4

    def send(value, ds, dt):
        pairs = []
        for s in range(secs):
            for t in range(tiles):
                if 0 <= s + ds < secs and 0 <= t + dt < tiles:
                    pairs.append((s * tiles + t, (s + ds) * tiles + t + dt))
        return lax.ppermute(value, ("sec", "tile"), pairs)

    own = features.transpose(0, 2, 1, 3)
    prev = send(own, 1, 0)
    head, tail = own[:, :2], own[:, rows - 2:]
    top = jnp.concatenate([send(tail, 1, 1), send(tail, 0, 1)], axis=0)
    bot = jnp.concatenate([send(head, 1, -1), send(head, 0, -1)], axis=0)
    w1, w1t, b1, w2, w2t = weights_of(first_kernel, first_bias, second_kernel)

    vmem = pl.BlockSpec(memory_space=pltpu.VMEM)
    smem = pl.BlockSpec(memory_space=pltpu.SMEM)
    voted, grad = pl.pallas_call(
        compute_kernel,
        out_shape=(
            jax.ShapeDtypeStruct((count, 2, rows, cols), F32),
            jax.ShapeDtypeStruct((2 * count, xrows, chans, cols), F32),
        ),
        in_specs=[vmem] * 5 + [smem] * 2 + [vmem] * 5 + [smem],
        out_specs=(vmem, vmem),
        scratch_shapes=[
            pltpu.VMEM((2 * count, 3 * chans, xrows * cols), BF),
            pltpu.VMEM((2 * count, 2 * width, hrows * cols), F32),
            pltpu.VMEM((LAGS * width, hrows * cols), BF),
            pltpu.VMEM((80, hrows * cols), F32),
            pltpu.VMEM((rows, 8, cols), F32),
            pltpu.VMEM((xrows, 8, cols), F32),
            pltpu.VMEM((80, hrows * cols), BF),
            pltpu.VMEM((count, LAGS * width, hrows * cols), F32),
            pltpu.VMEM((2 * width, hrows * cols), BF),
            pltpu.VMEM((9 * chans, hrows * cols), F32),
        ],
        compiler_params=pltpu.CompilerParams(vmem_limit_bytes=48 * 1024 * 1024),
        cost_estimate=pl.CostEstimate(flops=3 * 10**9, bytes_accessed=6 * 10**6, transcendentals=0),
    )(prev, own, top, bot, vote_grad, sharpness, valid_rows, w1, w1t, b1, w2, w2t, second_bias)

    low = grad.astype(BF)
    back = send(low[:count, 2:2 + rows], -1, 0)
    upper = send(low[:count, :2], -1, -1).astype(F32) + send(low[count:, :2], 0, -1).astype(F32)
    lower = send(low[:count, 2 + rows:], -1, 1).astype(F32) + send(low[count:, 2 + rows:], 0, 1).astype(F32)
    inner = grad[count:, 2:2 + rows] + back.astype(F32)
    gap = jnp.zeros((count, rows - 4, chans, cols), F32)
    inner = inner + jnp.concatenate([lower, gap, upper], axis=1)
    return voted, inner.transpose(0, 2, 1, 3)


def solution(mesh):
    return jax.shard_map(
        body,
        mesh=mesh,
        in_specs=(
            P("sec", None, "tile", None),
            P("sec", None, "tile", None),
            P("sec"),
            P("sec"),
            P(),
            P(),
            P(),
            P(),
        ),
        out_specs=(P("sec", None, "tile", None), P("sec", None, "tile", None)),
        check_vma=False,
    )
```

profile of v0, /device:TPU:11, one launch (start us, length us, event | category | flops | bytes accessed | tf_op | source)
XLA Modules:
  0.0 54.1 jit_solution(8765087655100286483)
XLA Ops:
  0.6 0.0 copy-start
  0.6 0.0 copy-start.1
  0.7 0.0 copy-start.2
  0.7 0.0 copy-start.4
  0.7 0.0 copy-start.3
  0.7 1.1 %copy.24 = bf16[3,32,16,128]{3,1,2,0:T(8,128)(2,1)S(1)} copy(bf16[3,32,16,128]{3,2,1,0:T(8,128)(2,1)} %param.8) | data formatting | bytes 786432 | tf_op args[0]
  1.8 3.7 %collective-permute-start = (bf16[3,16,32,128]{3,2,1,0:T(8,128)(2,1)S(1)}, bf16[3,16,32,128]{3,2,1,0:T(8,128)(2,1)S(1)}, u32[]{:S(2)}, u32[]{:S(2)}) collective-permute-start(bf16[3,16,32,128]{3,2,1,0:T(8,128)(2,1)S(1)} %bitcast.17), channel_id=1, source_target_pairs={{0,4},{1,5},{2,6},{3,7},{4,8},{5,9},{6,10},{7,11},{8,12},{9,13},{1... | collective-permute-start | bytes 1179656 | tf_op jit(solution)/shard_map/ppermute | solution.py:179
  5.5 3.2 %collective-permute-start.2 = (bf16[3,2,32,128]{3,2,1,0:T(8,128)(2,1)S(1)}, bf16[3,2,32,128]{3,2,1,0:T(8,128)(2,1)S(1)}, u32[]{:S(2)}, u32[]{:S(2)}) collective-permute-start(bf16[3,2,32,128]{3,2,1,0:T(8,128)(2,1)S(1)} %get-tuple-element.15), channel_id=1, source_target_pairs={{0,1},{1,2},{2,3},{4,5},{5,6},{6,7},{8,9},{9,10},{10,11},{12,13},{... | collective-permute-start | bytes 147464 | tf_op jit(solution)/shard_map/ppermute | solution.py:179
  8.7 3.2 %collective-permute-start.1 = (bf16[3,2,32,128]{3,2,1,0:T(8,128)(2,1)S(1)}, bf16[3,2,32,128]{3,2,1,0:T(8,128)(2,1)S(1)}, u32[]{:S(2)}, u32[]{:S(2)}) collective-permute-start(bf16[3,2,32,128]{3,2,1,0:T(8,128)(2,1)S(1)} %get-tuple-element.15), channel_id=1, source_target_pairs={{0,5},{1,6},{2,7},{4,9},{5,10},{6,11},{8,13},{9,14},{10,15},{12,17... | collective-permute-start | bytes 147464 | tf_op jit(solution)/shard_map/ppermute | solution.py:179
  11.9 2.1 %collective-permute-start.4 = (bf16[3,2,32,128]{3,2,1,0:T(8,128)(2,1)S(1)}, bf16[3,2,32,128]{3,2,1,0:T(8,128)(2,1)S(1)}, u32[]{:S(2)}, u32[]{:S(2)}) collective-permute-start(bf16[3,2,32,128]{3,2,1,0:T(8,128)(2,1)S(1)} %get-tuple-element.14), channel_id=1, source_target_pairs={{1,0},{2,1},{3,2},{5,4},{6,5},{7,6},{9,8},{10,9},{11,10},{13,12},{... | collective-permute-start | bytes 147464 | tf_op jit(solution)/shard_map/ppermute | solution.py:179
  14.0 2.5 %collective-permute-start.3 = (bf16[3,2,32,128]{3,2,1,0:T(8,128)(2,1)S(1)}, bf16[3,2,32,128]{3,2,1,0:T(8,128)(2,1)S(1)}, u32[]{:S(2)}, u32[]{:S(2)}) collective-permute-start(bf16[3,2,32,128]{3,2,1,0:T(8,128)(2,1)S(1)} %get-tuple-element.14), channel_id=1, source_target_pairs={{1,4},{2,5},{3,6},{5,8},{6,9},{7,10},{9,12},{10,13},{11,14},{13,16... | collective-permute-start | bytes 147464 | tf_op jit(solution)/shard_map/ppermute | solution.py:179
  16.5 0.7 %copy.19 = bf16[3,3,2,64]{3,2,1,0:T(2,128)(2,1)S(1)} copy(bf16[3,3,2,64]{3,2,0,1:T(2,128)(2,1)} %bitcast.24) | data formatting | bytes 4608 | tf_op jit(solution)/shard_map/transpose | solution.py:157
  17.3 0.1 mul.24
  17.4 0.1 mul.25
  17.4 0.1 mul.26
  17.5 1.0 %copy.16 = bf16[3,3,64,64]{2,3,1,0:T(8,128)(2,1)S(1)} copy(bf16[3,3,64,64]{3,2,1,0:T(8,128)(2,1)} %param.12) | data formatting | bytes 147456 | tf_op args[4]
  18.6 0.1 copy.17
  18.7 0.1 reshape.32
  18.9 0.1 copy.21.w1
  19.0 0.1 copy.18
  19.1 0.1 reshape.33.w1t
  19.2 0.1 copy.20
  19.3 0.0 collective-permute-done.2
  19.4 0.0 collective-permute-done.1
  19.4 0.0 collective-permute-done.4
  19.4 0.2 collective-permute-done.3
  19.6 0.0 collective-permute-done.prev
  19.6 0.0 copy-done.4
  19.6 0.1 broadcast_in_dim.4.b1
  19.7 0.0 copy-done
  19.7 0.0 copy-done.1
  19.7 0.0 copy-done.2
  19.7 0.0 copy-done.3
  19.7 10.7 %shard_map.95 = (f32[3,2,16,128]{3,2,1,0:T(8,128)}, f32[6,20,32,128]{3,2,1,0:T(8,128)S(1)}) custom-call(bf16[3,16,32,128]{3,2,1,0:T(8,128)(2,1)S(1)} %collective-permute-done.prev, bf16[3,16,32,128]{3,2,1,0:T(8,128)(2,1)S(1)} %bitcast.19, bf16[6,2,32,128]{3,2,1,0:T(8,128)(2,1)S(1)} %pad_maximum_fusion.top, ...), custom_call_target="tpu_custom_call" | custom-call | flops 3000000000 | bytes 6000000 | tf_op jit(solution)/shard_map/pallas_call | solution.py:190
  30.3 0.2 convert_element_type.28
  30.6 2.3 %collective-permute-start.9 = (bf16[3,2,32,128]{3,2,1,0:T(8,128)(2,1)S(1)}, bf16[3,2,32,128]{3,2,1,0:T(8,128)(2,1)S(1)}, u32[]{:S(2)}, u32[]{:S(2)}) collective-permute-start(bf16[3,2,32,128]{3,2,1,0:T(8,128)(2,1)S(1)} %get-tuple-element.11), channel_id=1, source_target_pairs={{1,0},{2,1},{3,2},{5,4},{6,5},{7,6},{9,8},{10,9},{11,10},{13,12},{... | collective-permute-start | bytes 147464 | tf_op jit(solution)/shard_map/ppermute | solution.py:179
  32.9 1.9 %collective-permute-start.8 = (bf16[3,2,32,128]{3,2,1,0:T(8,128)(2,1)S(1)}, bf16[3,2,32,128]{3,2,1,0:T(8,128)(2,1)S(1)}, u32[]{:S(2)}, u32[]{:S(2)}) collective-permute-start(bf16[3,2,32,128]{3,2,1,0:T(8,128)(2,1)S(1)} %get-tuple-element.12), channel_id=1, source_target_pairs={{5,0},{6,1},{7,2},{9,4},{10,5},{11,6},{13,8},{14,9},{15,10},{17,12... | collective-permute-start | bytes 147464 | tf_op jit(solution)/shard_map/ppermute | solution.py:179
  34.9 0.1 pad.6.clone
  35.0 4.3 %collective-permute-start.7 = (bf16[3,2,32,128]{3,2,1,0:T(8,128)(2,1)S(1)}, bf16[3,2,32,128]{3,2,1,0:T(8,128)(2,1)S(1)}, u32[]{:S(2)}, u32[]{:S(2)}) collective-permute-start(bf16[3,2,32,128]{3,2,1,0:T(8,128)(2,1)S(1)} %get-tuple-element.13), channel_id=1, source_target_pairs={{0,1},{1,2},{2,3},{4,5},{5,6},{6,7},{8,9},{9,10},{10,11},{12,13},{... | collective-permute-start | bytes 147464 | tf_op jit(solution)/shard_map/ppermute | solution.py:179
  39.3 3.3 %collective-permute-start.6 = (bf16[3,2,32,128]{3,2,1,0:T(8,128)(2,1)S(1)}, bf16[3,2,32,128]{3,2,1,0:T(8,128)(2,1)S(1)}, u32[]{:S(2)}, u32[]{:S(2)}) collective-permute-start(bf16[3,2,32,128]{3,2,1,0:T(8,128)(2,1)S(1)} %get-tuple-element.10), channel_id=1, source_target_pairs={{4,1},{5,2},{6,3},{8,5},{9,6},{10,7},{12,9},{13,10},{14,11},{16,13... | collective-permute-start | bytes 147464 | tf_op jit(solution)/shard_map/ppermute | solution.py:179
  42.6 1.9 %collective-permute-start.5 = (bf16[3,16,32,128]{3,2,1,0:T(8,128)(2,1)S(1)}, bf16[3,16,32,128]{3,2,1,0:T(8,128)(2,1)S(1)}, u32[]{:S(2)}, u32[]{:S(2)}) collective-permute-start(bf16[3,16,32,128]{3,2,1,0:T(8,128)(2,1)S(1)} %slice.34), channel_id=1, source_target_pairs={{4,0},{5,1},{6,2},{7,3},{8,4},{9,5},{10,6},{11,7},{12,8},{13,9},{1... | collective-permute-start | bytes 1179656 | tf_op jit(solution)/shard_map/ppermute | solution.py:179
  44.5 0.0 collective-permute-done.9
  44.5 0.0 collective-permute-done.8
  44.6 0.0 collective-permute-done.7
  44.6 2.4 %collective-permute-done.6 = bf16[3,2,32,128]{3,2,1,0:T(8,128)(2,1)S(1)} collective-permute-done((bf16[3,2,32,128]{3,2,1,0:T(8,128)(2,1)S(1)}, bf16[3,2,32,128]{3,2,1,0:T(8,128)(2,1)S(1)}, u32[]{:S(2)}, u32[]{:S(2)}) %collective-permute-start.6) | collective-permute-done | bytes 49184 | tf_op jit(solution)/shard_map/ppermute | solution.py:179
  47.0 5.6 %collective-permute-done.5 = bf16[3,16,32,128]{3,2,1,0:T(8,128)(2,1)S(1)} collective-permute-done((bf16[3,16,32,128]{3,2,1,0:T(8,128)(2,1)S(1)}, bf16[3,16,32,128]{3,2,1,0:T(8,128)(2,1)S(1)}, u32[]{:S(2)}, u32[]{:S(2)}) %collective-permute-start.5) | collective-permute-done | bytes 393248 | tf_op jit(solution)/shard_map/ppermute | solution.py:179
  52.6 0.2 fusion
  52.8 1.3 %copy.22 = f32[3,32,16,128]{3,2,1,0:T(8,128)} copy(f32[3,32,16,128]{3,1,2,0:T(8,128)S(1)} %fusion) | data formatting | bytes 1572864
  (12 shorter events, 0.1 us)
Async XLA Ops:
  0.6 19.0 %copy-start = (f32[3,2,16,128]{3,2,1,0:T(8,128)S(1)}, f32[3,2,16,128]{3,2,1,0:T(8,128)}, u32[]{:S(2)}) copy-start(f32[3,2,16,128]{3,2,1,0:T(8,128)} %cot.1) | copy-start | bytes 147460
  0.6 19.0 %copy-start.1 = (f32[3]{0:T(128)S(1)}, f32[3]{0:T(128)}, u32[]{:S(2)}) copy-start(f32[3]{0:T(128)} %sharp.1) | copy-start | bytes 40
  0.7 19.0 %copy-start.2 = (s32[3]{0:T(128)S(1)}, s32[3]{0:T(128)}, u32[]{:S(2)}) copy-start(s32[3]{0:T(128)} %valid.1) | copy-start | bytes 40
  0.7 18.9 %copy-start.4 = (f32[64]{0:T(128)S(1)}, f32[64]{0:T(128)}, u32[]{:S(2)}) copy-start(f32[64]{0:T(128)} %param.13) | copy-start | bytes 772
  0.7 19.0 %copy-start.3 = (f32[2]{0:T(128)S(1)}, f32[2]{0:T(128)}, u32[]{:S(2)}) copy-start(f32[2]{0:T(128)} %b2.1) | copy-start | bytes 28
  1.8 17.8 %collective-permute-start = (bf16[3,16,32,128]{3,2,1,0:T(8,128)(2,1)S(1)}, bf16[3,16,32,128]{3,2,1,0:T(8,128)(2,1)S(1)}, u32[]{:S(2)}, u32[]{:S(2)}) collective-permute-start(bf16[3,16,32,128]{3,2,1,0:T(8,128)(2,1)S(1)} %bitcast.17), channel_id=1, source_target_pairs={{0,4},{1,5},{2,6},{3,7},{4,8},{5,9},{6,10},{7,11},{8,12},{9,13},{1... | collective-permute-start | bytes 1179656 | tf_op jit(solution)/shard_map/ppermute | solution.py:179
  5.5 13.8 %collective-permute-start.2 = (bf16[3,2,32,128]{3,2,1,0:T(8,128)(2,1)S(1)}, bf16[3,2,32,128]{3,2,1,0:T(8,128)(2,1)S(1)}, u32[]{:S(2)}, u32[]{:S(2)}) collective-permute-start(bf16[3,2,32,128]{3,2,1,0:T(8,128)(2,1)S(1)} %get-tuple-element.15), channel_id=1, source_target_pairs={{0,1},{1,2},{2,3},{4,5},{5,6},{6,7},{8,9},{9,10},{10,11},{12,13},{... | collective-permute-start | bytes 147464 | tf_op jit(solution)/shard_map/ppermute | solution.py:179
  8.7 10.6 %collective-permute-start.1 = (bf16[3,2,32,128]{3,2,1,0:T(8,128)(2,1)S(1)}, bf16[3,2,32,128]{3,2,1,0:T(8,128)(2,1)S(1)}, u32[]{:S(2)}, u32[]{:S(2)}) collective-permute-start(bf16[3,2,32,128]{3,2,1,0:T(8,128)(2,1)S(1)} %get-tuple-element.15), channel_id=1, source_target_pairs={{0,5},{1,6},{2,7},{4,9},{5,10},{6,11},{8,13},{9,14},{10,15},{12,17... | collective-permute-start | bytes 147464 | tf_op jit(solution)/shard_map/ppermute | solution.py:179
  11.9 7.4 %collective-permute-start.4 = (bf16[3,2,32,128]{3,2,1,0:T(8,128)(2,1)S(1)}, bf16[3,2,32,128]{3,2,1,0:T(8,128)(2,1)S(1)}, u32[]{:S(2)}, u32[]{:S(2)}) collective-permute-start(bf16[3,2,32,128]{3,2,1,0:T(8,128)(2,1)S(1)} %get-tuple-element.14), channel_id=1, source_target_pairs={{1,0},{2,1},{3,2},{5,4},{6,5},{7,6},{9,8},{10,9},{11,10},{13,12},{... | collective-permute-start | bytes 147464 | tf_op jit(solution)/shard_map/ppermute | solution.py:179
  14.0 5.5 %collective-permute-start.3 = (bf16[3,2,32,128]{3,2,1,0:T(8,128)(2,1)S(1)}, bf16[3,2,32,128]{3,2,1,0:T(8,128)(2,1)S(1)}, u32[]{:S(2)}, u32[]{:S(2)}) collective-permute-start(bf16[3,2,32,128]{3,2,1,0:T(8,128)(2,1)S(1)} %get-tuple-element.14), channel_id=1, source_target_pairs={{1,4},{2,5},{3,6},{5,8},{6,9},{7,10},{9,12},{10,13},{11,14},{13,16... | collective-permute-start | bytes 147464 | tf_op jit(solution)/shard_map/ppermute | solution.py:179
  30.6 13.9 %collective-permute-start.9 = (bf16[3,2,32,128]{3,2,1,0:T(8,128)(2,1)S(1)}, bf16[3,2,32,128]{3,2,1,0:T(8,128)(2,1)S(1)}, u32[]{:S(2)}, u32[]{:S(2)}) collective-permute-start(bf16[3,2,32,128]{3,2,1,0:T(8,128)(2,1)S(1)} %get-tuple-element.11), channel_id=1, source_target_pairs={{1,0},{2,1},{3,2},{5,4},{6,5},{7,6},{9,8},{10,9},{11,10},{13,12},{... | collective-permute-start | bytes 147464 | tf_op jit(solution)/shard_map/ppermute | solution.py:179
  32.9 11.6 %collective-permute-start.8 = (bf16[3,2,32,128]{3,2,1,0:T(8,128)(2,1)S(1)}, bf16[3,2,32,128]{3,2,1,0:T(8,128)(2,1)S(1)}, u32[]{:S(2)}, u32[]{:S(2)}) collective-permute-start(bf16[3,2,32,128]{3,2,1,0:T(8,128)(2,1)S(1)} %get-tuple-element.12), channel_id=1, source_target_pairs={{5,0},{6,1},{7,2},{9,4},{10,5},{11,6},{13,8},{14,9},{15,10},{17,12... | collective-permute-start | bytes 147464 | tf_op jit(solution)/shard_map/ppermute | solution.py:179
  35.0 9.6 %collective-permute-start.7 = (bf16[3,2,32,128]{3,2,1,0:T(8,128)(2,1)S(1)}, bf16[3,2,32,128]{3,2,1,0:T(8,128)(2,1)S(1)}, u32[]{:S(2)}, u32[]{:S(2)}) collective-permute-start(bf16[3,2,32,128]{3,2,1,0:T(8,128)(2,1)S(1)} %get-tuple-element.13), channel_id=1, source_target_pairs={{0,1},{1,2},{2,3},{4,5},{5,6},{6,7},{8,9},{9,10},{10,11},{12,13},{... | collective-permute-start | bytes 147464 | tf_op jit(solution)/shard_map/ppermute | solution.py:179
  39.3 7.7 %collective-permute-start.6 = (bf16[3,2,32,128]{3,2,1,0:T(8,128)(2,1)S(1)}, bf16[3,2,32,128]{3,2,1,0:T(8,128)(2,1)S(1)}, u32[]{:S(2)}, u32[]{:S(2)}) collective-permute-start(bf16[3,2,32,128]{3,2,1,0:T(8,128)(2,1)S(1)} %get-tuple-element.10), channel_id=1, source_target_pairs={{4,1},{5,2},{6,3},{8,5},{9,6},{10,7},{12,9},{13,10},{14,11},{16,13... | collective-permute-start | bytes 147464 | tf_op jit(solution)/shard_map/ppermute | solution.py:179
  42.6 10.0 %collective-permute-start.5 = (bf16[3,16,32,128]{3,2,1,0:T(8,128)(2,1)S(1)}, bf16[3,16,32,128]{3,2,1,0:T(8,128)(2,1)S(1)}, u32[]{:S(2)}, u32[]{:S(2)}) collective-permute-start(bf16[3,16,32,128]{3,2,1,0:T(8,128)(2,1)S(1)} %slice.34), channel_id=1, source_target_pairs={{4,0},{5,1},{6,2},{7,3},{8,4},{9,5},{10,6},{11,7},{12,8},{13,9},{1... | collective-permute-start | bytes 1179656 | tf_op jit(solution)/shard_map/ppermute | solution.py:179
where the time goes:
time: 54.9 us; the launch traced here: 54.1 us
  starting transfers between devices  28.5 us (52%)
  Pallas kernels  10.7 us (19%)
  waiting for transfers between devices  8.21 us (15%)
  local copies, waits for them, and re-layouts  5.43 us (10%)
  between operations  0.96 us (2%)
    ppermute x10, starting transfers between devices, send(): return lax.ppermute(value, ('sec', 'tile'), pairs)  28.5 us
    pallas_call x1, Pallas kernels, body(): pl.pallas_call(compute_kernel, out_shape=(jax.ShapeDtypeStruct((count, 2,...  10.7 us
    ppermute x10, waiting for transfers between devices, send(): return lax.ppermute(value, ('sec', 'tile'), pairs)  8.21 us
    unnamed x13, local copies, waits for them, and re-layouts  3.53 us
  transfers between devices with their start and end apart: 10, of which 3 were waited for; matrix products, arithmetic and copies ran while one was open for 5% of the time, Pallas kernels for 0%

commit v1 on v0

v1 whole, which is shorter than its diff:
```python
import functools

import jax
import jax.numpy as jnp
from jax import lax
from jax.experimental import pallas as pl
from jax.experimental.pallas import tpu as pltpu
from jax.sharding import PartitionSpec as P

LAGS = 3
BF = jnp.bfloat16
F32 = jnp.float32


def shifted(value, step):
    lanes = value.shape[-1]
    lane = lax.broadcasted_iota(jnp.int32, value.shape, value.ndim - 1)
    rolled = pltpu.roll(value, step % lanes, value.ndim - 1)
    return jnp.where(lane == (0 if step == 1 else lanes - 1), 0.0, rolled)


def kernel(
    own, cot, sharp, valid, w1, w1t, b1, w2, w2t, b2,
    voted, grad,
    prev, top, bot, xs, ab, hid, tap, fld, dfl, dst, gcur, gear, mix,
    outer, rims, back, fold,
    fsend, frecv, bsend, brecv,
):
    count, rows, chans, cols = own.shape
    hrows, xrows = rows + 2, rows + 4
    width = b1.shape[0]
    sec, tile = lax.axis_index("sec"), lax.axis_index("tile")
    secs, tiles = lax.axis_size("sec"), lax.axis_size("tile")

    def exists(ds, dt):
        there = jnp.bool_(True)
        if ds:
            there = sec > 0 if ds < 0 else sec < secs - 1
        if dt:
            other = tile > 0 if dt < 0 else tile < tiles - 1
            there = jnp.logical_and(there, other) if ds else other
        return there

    def device(ds, dt):
        return (lax.rem(sec + ds + secs, secs), lax.rem(tile + dt + tiles, tiles))

    around = [(ds, dt) for ds in (-1, 0, 1) for dt in (-1, 0, 1) if ds or dt]
    barrier = pltpu.get_barrier_semaphore()
    for ds, dt in around:
        @pl.when(exists(ds, dt))
        def _():
            pl.semaphore_signal(
                barrier, inc=1, device_id=device(ds, dt), device_id_type=pl.DeviceIdType.MESH
            )

    def copy(source, target, send, recv, ds, dt):
        return pltpu.make_async_remote_copy(
            src_ref=source, dst_ref=target, send_sem=send, recv_sem=recv,
            device_id=device(ds, dt), device_id_type=pl.DeviceIdType.MESH,
        )

    def start(item):
        @pl.when(exists(item[1], item[2]))
        def _():
            item[0].start()

    def arrive(item):
        @pl.when(exists(-item[1], -item[2]))
        def _():
            item[0].wait_recv()

    def leave(item):
        @pl.when(exists(item[1], item[2]))
        def _():
            item[0].wait_send()

    head, tail = own.at[:, 0:2], own.at[:, rows - 2:rows]
    plan = [
        (tail, top.at[count:2 * count], 0, 1),
        (head, bot.at[count:2 * count], 0, -1),
        (tail, top.at[0:count], 1, 1),
        (head, bot.at[0:count], 1, -1),
        (own, prev, 1, 0),
    ]
    ahead = [
        (copy(a, b, fsend.at[i], frecv.at[i], ds, dt), ds, dt) for i, (a, b, ds, dt) in enumerate(plan)
    ]

    def returns(t):
        parts = [(slice(2, 2 + rows), back.at[t], -1, 0)]
        parts.append((slice(0, 2), fold.at[0, t], -1, -1))
        parts.append((slice(2 + rows, xrows), fold.at[1, t], -1, 1))
        return [
            (copy(outer.at[t, at], to, bsend.at[i, t], brecv.at[i, t], ds, dt), ds, dt)
            for i, (at, to, ds, dt) in enumerate(parts)
        ]

    def edges(t):
        return [
            (
                copy(rims.at[i, t], fold.at[i, count + t], bsend.at[3 + i, t], brecv.at[3 + i, t], 0, dt),
                0,
                dt,
            )
            for i, dt in enumerate((-1, 1))
        ]

    def lane(row, num=1):
        return slice(row * cols, (row + num) * cols)

    for i, (_, to, ds, dt) in enumerate(plan):
        @pl.when(jnp.logical_not(exists(-ds, -dt)))
        def _():
            to[...] = jnp.zeros(to.shape, BF)

    gear[0:2] = jnp.zeros((2,) + gear.shape[1:], F32)
    gear[2 * count - 1] = jnp.zeros(gear.shape[1:], F32)
    dfl[...] = jnp.zeros_like(dfl)

    near = lambda low, high: low.astype(jnp.int32) + high.astype(jnp.int32) + 1
    pl.semaphore_wait(barrier, near(sec > 0, sec < secs - 1) * near(tile > 0, tile < tiles - 1) - 1)
    for item in ahead:
        start(item)

    def place(section, row, value):
        wide = value.astype(F32)
        xs[section, 0:chans, lane(row)] = shifted(wide, 1).astype(BF)
        xs[section, chans:2 * chans, lane(row)] = value
        xs[section, 2 * chans:3 * chans, lane(row)] = shifted(wide, -1).astype(BF)

    def first(s, low):
        for r in range(0, hrows, 2):
            stack = jnp.concatenate([xs[s, :, lane(r + dy, 2)] for dy in range(3)], axis=0)
            ab[s, low:, lane(r, 2)] = jnp.dot(w1[low:, :], stack, preferred_element_type=F32)

    def place_own(s, _):
        for r in range(rows):
            place(s + count, r + 2, own[s, r])
        return 0

    def place_rim(s, _):
        for r in range(2):
            place(s, r, top[s, r])
            place(s, rows + 2 + r, bot[s, r])
        first(s, 0)
        return 0

    def place_prev(s, _):
        for r in range(rows):
            place(s, r + 2, prev[s, r])
        for r in range(2):
            place(s, r, top[s, r])
            place(s, rows + 2 + r, bot[s, r])
        first(s, width)
        return 0

    lax.fori_loop(0, count, place_own, 0)
    for item in ahead[:2]:
        arrive(item)
    lax.fori_loop(count, 2 * count, place_rim, 0)
    for item in ahead[2:]:
        arrive(item)
    lax.fori_loop(0, count, place_prev, 0)

    def pulled_row(slot, x):
        parts = []
        for dx in range(3):
            terms = []
            for dy in range(3):
                if 0 <= x - dy < hrows:
                    at = (dx * 3 + dy) * chans
                    terms.append(mix[slot, at:at + chans, lane(x - dy)])
            parts.append(sum(terms))
        return parts[1] + shifted(parts[0], -1) + shifted(parts[2], 1)

    def section(s, _):
        for k in range(LAGS):
            for r in range(hrows):
                total = ab[s + count, 0:width, lane(r)] + ab[s + count - 1 - k, width:, lane(r)]
                hid[k * width:(k + 1) * width, lane(r)] = jnp.maximum(total + b1[...], 0.0).astype(BF)

        @pl.when(tile == 0)
        def _():
            hid[:, lane(0)] = jnp.zeros((LAGS * width, cols), BF)

        @pl.when(tile == tiles - 1)
        def _():
            hid[:, lane(hrows - 1)] = jnp.zeros((LAGS * width, cols), BF)

        tap[...] = jnp.dot(w2[...], hid[...], preferred_element_type=F32)
        for r in range(rows):
            parts = []
            for dx in range(3):
                at = [(dx * 3 + dy) * 8 for dy in range(3)]
                parts.append(sum(tap[at[dy]:at[dy] + 8, lane(r + dy)] for dy in range(3)))
            fld[r] = parts[1] + shifted(parts[0], 1) + shifted(parts[2], -1)

        f = [[fld[:, 2 * k + c, :] + b2[c] for c in range(2)] for k in range(LAGS)]
        dist = {}
        for k in range(LAGS):
            for j in range(k):
                dist[k, j] = dist[j, k] = sum((f[k][c] - f[j][c]) ** 2 for c in range(2))
        logits = [-sharp[s] * sum(dist[k, j] for j in range(LAGS) if j != k) for k in range(LAGS)]
        peak = jnp.maximum(jnp.maximum(logits[0], logits[1]), logits[2])
        expo = [jnp.exp(v - peak) for v in logits]
        norm = expo[0] + expo[1] + expo[2]
        weight = [e / norm for e in expo]
        row = lax.broadcasted_iota(jnp.int32, (rows, cols), 0) + tile * rows
        live = row < valid[s]
        g = [jnp.where(live, cot[s, c], 0.0) for c in range(2)]
        for c in range(2):
            voted[s, c] = sum(weight[k] * f[k][c] for k in range(LAGS))
        dw = [g[0] * f[k][0] + g[1] * f[k][1] for k in range(LAGS)]
        mean = sum(weight[k] * dw[k] for k in range(LAGS))
        q = [-sharp[s] * weight[k] * (dw[k] - mean) for k in range(LAGS)]
        for k in range(LAGS):
            for c in range(2):
                pulled = sum((q[k] + q[j]) * (f[k][c] - f[j][c]) for j in range(LAGS) if j != k)
                dfl[2:2 + rows, 2 * k + c, :] = weight[k] * g[c] + 2.0 * pulled

        zero = jnp.zeros((8, cols), F32)
        moved = [[shifted(dfl[r], -1), dfl[r], shifted(dfl[r], 1)] for r in range(xrows)]
        for r in range(hrows):
            taps = [moved[r - dy + 2][dx] for dx in range(3) for dy in range(3)]
            dst[:, lane(r)] = jnp.concatenate(taps + [zero], axis=0).astype(BF)
        for r in range(0, hrows, 2):
            pulled = jnp.dot(w2t[...], dst[:, lane(r, 2)], preferred_element_type=F32)
            pulled = jnp.where(hid[:, lane(r, 2)].astype(F32) > 0.0, pulled, 0.0)
            lag = [pulled[k * width:(k + 1) * width] for k in range(LAGS)]
            gcur[s, 0:width, lane(r, 2)] = (lag[0] + lag[1] + lag[2]).astype(BF)
            gear[s + count - 1, :, lane(r, 2)] = lag[0]
            for k in range(1, LAGS):
                gear[s + count - 1 - k, :, lane(r, 2)] += lag[k]

        for r in range(0, hrows, 2):
            mix[0, :, lane(r, 2)] = jnp.dot(
                w1t[:, width:], gear[s, :, lane(r, 2)].astype(BF), preferred_element_type=F32
            )
        for x in range(xrows):
            outer[s, x] = pulled_row(0, x).astype(BF)
        for item in returns(s):
            start(item)
        return 0

    lax.fori_loop(0, count, section, 0)

    def chunk(t, r):
        gcur[t, width:, lane(r, 2)] = gear[t + count, :, lane(r, 2)].astype(BF)
        mix[t, :, lane(r, 2)] = jnp.dot(w1t[...], gcur[t, :, lane(r, 2)], preferred_element_type=F32)

    def own_edge(t, _):
        chunk(t, 0)
        chunk(t, hrows - 2)
        for i in range(2):
            for r in range(2):
                rims[i, t, r] = pulled_row(t, r + i * (xrows - 2)).astype(BF)
        for item in edges(t):
            start(item)
        return 0

    def own_inner(t, _):
        for r in range(2, hrows - 2, 2):
            chunk(t, r)
        for x in range(2, 2 + rows):
            grad[t, x - 2] = pulled_row(t, x)
        return 0

    lax.fori_loop(0, count, own_edge, 0)
    lax.fori_loop(0, count, own_inner, 0)

    for i, (source, ds, dt) in enumerate(((back, -1, 0), (fold, -1, -1), (fold, -1, 1), (fold, 0, -1), (fold, 0, 1))):
        @pl.when(jnp.logical_not(exists(-ds, -dt)))
        def _():
            if i == 0:
                back[...] = jnp.zeros(back.shape, BF)
            else:
                at = 0 if i < 3 else count
                fold[(i - 1) % 2, at:at + count] = jnp.zeros((count,) + fold.shape[2:], BF)

    tails = [item for t in range(count) for item in returns(t) + edges(t)]
    for item in tails:
        arrive(item)

    def finish(t, _):
        total = [back[t, r].astype(F32) for r in range(rows)]
        for r in range(2):
            total[rows - 2 + r] += fold[0, t, r].astype(F32) + fold[0, t + count, r].astype(F32)
            total[r] += fold[1, t, r].astype(F32) + fold[1, t + count, r].astype(F32)
        for r in range(rows):
            grad[t, r] += total[r]
        return 0

    lax.fori_loop(0, count, finish, 0)
    for item in ahead + tails:
        leave(item)


def weights_of(first_kernel, first_bias, second_kernel):
    width, chans = first_kernel.shape[2], first_kernel.shape[3] // 2
    split = first_kernel.reshape(3, 3, width, 2, chans)
    w1 = split.transpose(3, 2, 0, 1, 4).reshape(2 * width, 9 * chans)
    w1t = split.transpose(1, 0, 4, 3, 2).reshape(9 * chans, 2 * width)
    taps = second_kernel.transpose(1, 0, 2, 3).reshape(9, 1, 2, 1, width)
    eye = jnp.eye(LAGS, dtype=BF).reshape(1, LAGS, 1, LAGS, 1)
    w2 = (taps * eye).reshape(9, 2 * LAGS, LAGS * width)
    w2 = jnp.pad(w2, ((0, 1), (0, 8 - 2 * LAGS), (0, 0))).reshape(80, LAGS * width)
    b1 = jnp.broadcast_to(first_bias[:, None], (width, 128))
    return w1, w1t, b1, w2, w2.T


def body(
    features, vote_grad, sharpness, valid_rows, first_kernel, first_bias, second_kernel, second_bias
):
    count, chans, rows, cols = features.shape
    width = first_kernel.shape[2]
    hrows, xrows = rows + 2, rows + 4

    own = features.transpose(0, 2, 1, 3)
    w1, w1t, b1, w2, w2t = weights_of(first_kernel, first_bias, second_kernel)

    vmem = pl.BlockSpec(memory_space=pltpu.VMEM)
    smem = pl.BlockSpec(memory_space=pltpu.SMEM)
    voted, grad = pl.pallas_call(
        kernel,
        out_shape=(
            jax.ShapeDtypeStruct((count, 2, rows, cols), F32),
            jax.ShapeDtypeStruct((count, rows, chans, cols), F32),
        ),
        in_specs=[vmem] * 2 + [smem] * 2 + [vmem] * 5 + [smem],
        out_specs=(vmem, vmem),
        scratch_shapes=[
            pltpu.VMEM((count, rows, chans, cols), BF),
            pltpu.VMEM((2 * count, 2, chans, cols), BF),
            pltpu.VMEM((2 * count, 2, chans, cols), BF),
            pltpu.VMEM((2 * count, 3 * chans, xrows * cols), BF),
            pltpu.VMEM((2 * count, 2 * width, hrows * cols), F32),
            pltpu.VMEM((LAGS * width, hrows * cols), BF),
            pltpu.VMEM((80, hrows * cols), F32),
            pltpu.VMEM((rows, 8, cols), F32),
            pltpu.VMEM((xrows, 8, cols), F32),
            pltpu.VMEM((80, hrows * cols), BF),
            pltpu.VMEM((count, 2 * width, hrows * cols), BF),
            pltpu.VMEM((2 * count, width, hrows * cols), F32),
            pltpu.VMEM((count, 9 * chans, hrows * cols), F32),
            pltpu.VMEM((count, xrows, chans, cols), BF),
            pltpu.VMEM((2, count, 2, chans, cols), BF),
            pltpu.VMEM((count, rows, chans, cols), BF),
            pltpu.VMEM((2, 2 * count, 2, chans, cols), BF),
            pltpu.SemaphoreType.DMA((5,)),
            pltpu.SemaphoreType.DMA((5,)),
            pltpu.SemaphoreType.DMA((5, count)),
            pltpu.SemaphoreType.DMA((5, count)),
        ],
        compiler_params=pltpu.CompilerParams(
            vmem_limit_bytes=48 * 1024 * 1024, collective_id=0, has_side_effects=True
        ),
        cost_estimate=pl.CostEstimate(flops=3 * 10**9, bytes_accessed=6 * 10**6, transcendentals=0),
    )(own, vote_grad, sharpness, valid_rows, w1, w1t, b1, w2, w2t, second_bias)
    return voted, grad.transpose(0, 2, 1, 3)


def solution(mesh):
    return jax.shard_map(
        body,
        mesh=mesh,
        in_specs=(
            P("sec", None, "tile", None),
            P("sec", None, "tile", None),
            P("sec"),
            P("sec"),
            P(),
            P(),
            P(),
            P(),
        ),
        out_specs=(P("sec", None, "tile", None), P("sec", None, "tile", None)),
        check_vma=False,
    )
```

time: 54.9 us -> 30.2 us (0.55)
  starting transfers between devices: 28.5 us -> 0 us
  Pallas kernels: 10.7 us -> 22.7 us
  waiting for transfers between devices: 8.21 us -> 0 us
  local copies, waits for them, and re-layouts: 5.43 us -> 6.48 us
    ppermute x10 -> x0, starting transfers between devices: 28.5 us -> none  [send(): return lax.ppermute(value, ('sec', 'tile'), pairs)]
    pallas_call x1, Pallas kernels: 10.7 us -> 22.7 us  [body(): pl.pallas_call(kernel, out_shape=(jax.ShapeDtypeStruct((count, 2, rows, c...]
    ppermute x10 -> x0, waiting for transfers between devices: 8.21 us -> none  [send(): return lax.ppermute(value, ('sec', 'tile'), pairs)]
    unnamed x13 -> x18, local copies, waits for them, and re-layouts: 3.53 us -> 4.73 us
  transfers between devices with their start and end apart: 10 -> 0, of which waited for: 3 -> 0; matrix products, arithmetic and copies ran while one was open for 5% -> 0% of each run, Pallas kernels for 0% -> 0%
where the time goes in v1:
time: 30.2 us; the launch traced here: 30 us
  Pallas kernels  22.7 us (75%)
  local copies, waits for them, and re-layouts  6.48 us (21%)
  between operations  0.76 us (3%)
    pallas_call x1, Pallas kernels, body(): pl.pallas_call(kernel, out_shape=(jax.ShapeDtypeStruct((count, 2, rows, c...  22.7 us
    unnamed x18, local copies, waits for them, and re-layouts  4.73 us
    transpose x1, local copies, waits for them, and re-layouts, weights_of(): taps = second_kernel.transpose(1, 0, 2, 3).reshape(9, 1, 2, 1, width)  0.7 us

profile of v1, /device:TPU:11, one launch (start us, length us, event | category | flops | bytes accessed | tf_op | source)
XLA Modules:
  0.0 30.0 jit_solution(9513325207729652799)
XLA Ops:
  0.6 0.7 %copy.19 = bf16[3,3,2,64]{3,2,1,0:T(2,128)(2,1)S(1)} copy(bf16[3,3,2,64]{3,2,0,1:T(2,128)(2,1)} %bitcast.22) | data formatting | bytes 4608 | tf_op jit(solution)/shard_map/transpose | solution.py:303
  1.3 0.1 mul.25
  1.4 0.0 copy-start.6
  1.4 0.1 mul.26
  1.5 0.6 %copy-done.6 = f32[64]{0:T(128)S(1)} copy-done((f32[64]{0:T(128)S(1)}, f32[64]{0:T(128)}, u32[]{:S(2)}) %copy-start.6) | copy-done | bytes 280
  2.1 0.1 broadcast_in_dim.2.b1
  2.2 0.0 copy-start.5
  2.2 0.1 mul.24
  2.3 0.1 copy.20
  2.4 0.7 %copy-done.5 = bf16[3,3,64,64]{3,2,1,0:T(8,128)(2,1)S(1)} copy-done((bf16[3,3,64,64]{3,2,1,0:T(8,128)(2,1)S(1)}, bf16[3,3,64,64]{3,2,1,0:T(8,128)(2,1)}, u32[]{:S(2)}) %copy-start.5) | copy-done | bytes 73752
  3.1 0.1 copy.16
  3.2 0.1 copy.18
  3.4 0.1 reshape.33.w1t
  3.5 0.0 copy-start.4
  3.5 0.1 copy.17
  3.6 0.1 reshape.32
  3.7 0.1 copy.21.w1
  3.9 0.6 %copy-done.4 = bf16[3,32,16,128]{3,2,1,0:T(8,128)(2,1)S(1)} copy-done((bf16[3,32,16,128]{3,2,1,0:T(8,128)(2,1)S(1)}, bf16[3,32,16,128]{3,2,1,0:T(8,128)(2,1)}, u32[]{:S(2)}) %copy-start.4) | copy-done | bytes 393240
  4.5 0.0 copy-start
  4.5 0.1 copy.24
  4.6 0.0 copy-start.1
  4.6 0.0 copy-start.2
  4.6 0.0 copy-start.3
  4.6 0.7 %copy-done = f32[3,2,16,128]{3,2,1,0:T(8,128)S(1)} copy-done((f32[3,2,16,128]{3,2,1,0:T(8,128)S(1)}, f32[3,2,16,128]{3,2,1,0:T(8,128)}, u32[]{:S(2)}) %copy-start) | copy-done | bytes 49176
  5.3 0.0 copy-done.1
  5.3 0.0 copy-done.2
  5.3 0.0 copy-done.3
  5.3 22.7 %shard_map.95 = (f32[3,2,16,128]{3,2,1,0:T(8,128)S(1)}, f32[3,16,32,128]{3,2,1,0:T(8,128)S(1)}) custom-call(bf16[3,16,32,128]{3,2,1,0:T(8,128)(2,1)S(1)} %bitcast.17, f32[3,2,16,128]{3,2,1,0:T(8,128)S(1)} %copy-done, f32[3]{0:T(128)S(1)} %copy-done.1, s32[3]{0:T(128)S(1)} %copy-done.2, bf16[128,288]{1,0:T(8,128)(2,1)S(1)} %copy.21.w1, ...), custom_call_target="tpu_custom_call" | custom-call | flops 3000000000 | bytes 6000000 | tf_op jit(solution)/shard_map/pallas_call | solution.py:323
  28.0 1.3 %copy.22 = f32[3,32,16,128]{3,2,1,0:T(8,128)} copy(f32[3,32,16,128]{3,1,2,0:T(8,128)S(1)} %bitcast.16) | data formatting | bytes 1572864
  29.3 0.6 %copy.26 = f32[3,2,16,128]{3,2,1,0:T(8,128)} copy(f32[3,2,16,128]{3,2,1,0:T(8,128)S(1)} %get-tuple-element.12) | data formatting | bytes 98304
  (4 shorter events, 0.0 us)
Async XLA Ops:
  1.4 0.7 %copy-start.6 = (f32[64]{0:T(128)S(1)}, f32[64]{0:T(128)}, u32[]{:S(2)}) copy-start(f32[64]{0:T(128)} %param.13) | copy-start | bytes 772
  2.2 0.9 %copy-start.5 = (bf16[3,3,64,64]{3,2,1,0:T(8,128)(2,1)S(1)}, bf16[3,3,64,64]{3,2,1,0:T(8,128)(2,1)}, u32[]{:S(2)}) copy-start(bf16[3,3,64,64]{3,2,1,0:T(8,128)(2,1)} %param.12) | copy-start | bytes 221188
  3.5 1.0 %copy-start.4 = (bf16[3,32,16,128]{3,2,1,0:T(8,128)(2,1)S(1)}, bf16[3,32,16,128]{3,2,1,0:T(8,128)(2,1)}, u32[]{:S(2)}) copy-start(bf16[3,32,16,128]{3,2,1,0:T(8,128)(2,1)} %param.8) | copy-start | bytes 1179652
  4.5 0.8 %copy-start = (f32[3,2,16,128]{3,2,1,0:T(8,128)S(1)}, f32[3,2,16,128]{3,2,1,0:T(8,128)}, u32[]{:S(2)}) copy-start(f32[3,2,16,128]{3,2,1,0:T(8,128)} %cot.1) | copy-start | bytes 147460
  4.6 0.7 %copy-start.1 = (f32[3]{0:T(128)S(1)}, f32[3]{0:T(128)}, u32[]{:S(2)}) copy-start(f32[3]{0:T(128)} %sharp.1) | copy-start | bytes 40
  4.6 0.7 %copy-start.2 = (s32[3]{0:T(128)S(1)}, s32[3]{0:T(128)}, u32[]{:S(2)}) copy-start(s32[3]{0:T(128)} %valid.1) | copy-start | bytes 40
  4.6 0.7 %copy-start.3 = (f32[2]{0:T(128)S(1)}, f32[2]{0:T(128)}, u32[]{:S(2)}) copy-start(f32[2]{0:T(128)} %b2.1) | copy-start | bytes 28

commit v2 on v1

--- a/solution.py
+++ b/solution.py
@@ -20,15 +20,22 @@
 
 
 def kernel(
-    own, cot, sharp, valid, w1, w1t, b1, w2, w2t, b2,
+    own, sharp, valid, b2, cot_hbm, fk_hbm, sk_hbm, b1_hbm,
     voted, grad,
-    prev, top, bot, xs, ab, hid, tap, fld, dfl, dst, gcur, gear, mix,
+    cot, fk, sk, bias, w1, wcur, wear, b1, w2f, w2, w2t,
+    prev, top, bot, xs, ab, hid, tap, fld, dfl, dst, dhid, gcur, gear,
     outer, rims, back, fold,
-    fsend, frecv, bsend, brecv,
+    fsend, frecv, bsend, brecv, local,
 ):
     count, rows, chans, cols = own.shape
     hrows, xrows = rows + 2, rows + 4
     width = b1.shape[0]
+    loads = [
+        pltpu.make_async_copy(a, b, local.at[i])
+        for i, (a, b) in enumerate(((fk_hbm, fk), (sk_hbm, sk), (b1_hbm, bias), (cot_hbm, cot)))
+    ]
+    for item in loads:
+        item.start()
     sec, tile = lax.axis_index("sec"), lax.axis_index("tile")
     secs, tiles = lax.axis_size("sec"), lax.axis_size("tile")
 
@@ -80,8 +87,8 @@
         (head, bot.at[count:2 * count], 0, -1),
         (tail, top.at[0:count], 1, 1),
         (head, bot.at[0:count], 1, -1),
-        (own, prev, 1, 0),
     ]
+    plan += [(own.at[t], prev.at[t], 1, 0) for t in (count - 1, *range(count - 1))]
     ahead = [
         (copy(a, b, fsend.at[i], frecv.at[i], ds, dt), ds, dt) for i, (a, b, ds, dt) in enumerate(plan)
     ]
@@ -113,14 +120,38 @@
         def _():
             to[...] = jnp.zeros(to.shape, BF)
 
-    gear[0:2] = jnp.zeros((2,) + gear.shape[1:], F32)
-    gear[2 * count - 1] = jnp.zeros(gear.shape[1:], F32)
+    for ref in (dhid, gcur, gear):
+        for row in (0, hrows + 2):
+            ref[:, :, lane(row, 2)] = jnp.zeros(ref.shape[:2] + (2 * cols,), BF)
     dfl[...] = jnp.zeros_like(dfl)
+
+    for item in loads:
+        item.wait()
+    b1[...] = jnp.broadcast_to(bias[...], (128, width)).T
+    wide = [[fk[dy, dx].astype(F32) for dx in range(3)] for dy in range(3)]
+    for half in range(2):
+        at = slice(half * chans, (half + 1) * chans)
+        taps = [wide[dy][dx][:, at] for dy in range(3) for dx in range(3)]
+        w1[half * width:(half + 1) * width, :] = jnp.concatenate(taps, axis=1).astype(BF)
 
     near = lambda low, high: low.astype(jnp.int32) + high.astype(jnp.int32) + 1
     pl.semaphore_wait(barrier, near(sec > 0, sec < secs - 1) * near(tile > 0, tile < tiles - 1) - 1)
     for item in ahead:
         start(item)
+
+    for dx in range(3):
+        turned = [wide[dy][dx].T for dy in range(3)]
+        at = slice(dx * chans, (dx + 1) * chans)
+        wcur[at, :] = jnp.concatenate([v[:chans] for v in turned], axis=1).astype(BF)
+        wear[at, :] = jnp.concatenate([v[chans:] for v in turned], axis=1).astype(BF)
+    w2f[...] = jnp.zeros_like(w2f)
+    for dx in range(3):
+        for dy in range(3):
+            for k in range(LAGS):
+                at = (dx * 3 + dy) * 8 + 2 * k
+                w2f[at:at + 2, k * width:(k + 1) * width] = sk[dy, dx].astype(F32)
+    w2[...] = w2f[0:80, 0:LAGS * width].astype(BF)
+    w2t[...] = w2f[...].T[0:LAGS * width, 0:80].astype(BF)
 
     def place(section, row, value):
         wide = value.astype(F32)
@@ -158,22 +189,53 @@
     for item in ahead[:2]:
         arrive(item)
     lax.fori_loop(count, 2 * count, place_rim, 0)
-    for item in ahead[2:]:
-        arrive(item)
-    lax.fori_loop(0, count, place_prev, 0)
-
-    def pulled_row(slot, x):
-        parts = []
-        for dx in range(3):
-            terms = []
-            for dy in range(3):
-                if 0 <= x - dy < hrows:
-                    at = (dx * 3 + dy) * chans
-                    terms.append(mix[slot, at:at + chans, lane(x - dy)])
-            parts.append(sum(terms))
-        return parts[1] + shifted(parts[0], -1) + shifted(parts[2], 1)
-
-    def section(s, _):
+    def earlier(t):
+        terms = [(t + k - count, k - 1) for k in range(1, LAGS + 1) if 0 <= t + k - count < count]
+        if not terms:
+            return None
+        views = [lambda at, s=s, k=k: dhid[s, k * width:(k + 1) * width, at] for s, k in terms]
+        if len(views) == 1:
+            return views[0]
+        for r in range(2, hrows + 2, 2):
+            total = sum(view(lane(r, 2)).astype(F32) for view in views)
+            gear[t, :, lane(r, 2)] = total.astype(BF)
+        return lambda at: gear[t, :, at]
+
+    def pulled_rows(x, halves):
+        total = None
+        for weights, view in halves:
+            stack = jnp.concatenate([view(lane(x - dy + 2, 2)) for dy in range(3)], axis=0)
+            part = jnp.dot(weights[...], stack, preferred_element_type=F32)
+            total = part if total is None else total + part
+        rows_of = []
+        for i in range(2):
+            at = slice(i * cols, (i + 1) * cols)
+            tap_of = [total[dx * chans:(dx + 1) * chans, at] for dx in range(3)]
+            rows_of.append(tap_of[1] + shifted(tap_of[0], -1) + shifted(tap_of[2], 1))
+        return rows_of
+
+    def borrowed(t):
+        halves = [(wear, earlier(t))]
+        for x in range(0, xrows, 2):
+            for i, value in enumerate(pulled_rows(x, halves)):
+                outer[t, x + i] = value.astype(BF)
+        for item in returns(t):
+            start(item)
+
+    def section(i, _):
+        s = lax.rem(i + count - 1, count)
+
+        @pl.when(i == 0)
+        def _():
+            arrive(ahead[4])
+            place_prev(count - 1, 0)
+
+        @pl.when(i == 1)
+        def _():
+            for item in ahead[5:]:
+                arrive(item)
+            lax.fori_loop(0, count - 1, place_prev, 0)
+
         for k in range(LAGS):
             for r in range(hrows):
                 total = ab[s + count, 0:width, lane(r)] + ab[s + count - 1 - k, width:, lane(r)]
@@ -227,46 +289,36 @@
             pulled = jnp.dot(w2t[...], dst[:, lane(r, 2)], preferred_element_type=F32)
             pulled = jnp.where(hid[:, lane(r, 2)].astype(F32) > 0.0, pulled, 0.0)
             lag = [pulled[k * width:(k + 1) * width] for k in range(LAGS)]
-            gcur[s, 0:width, lane(r, 2)] = (lag[0] + lag[1] + lag[2]).astype(BF)
-            gear[s + count - 1, :, lane(r, 2)] = lag[0]
-            for k in range(1, LAGS):
-                gear[s + count - 1 - k, :, lane(r, 2)] += lag[k]
-
-        for r in range(0, hrows, 2):
-            mix[0, :, lane(r, 2)] = jnp.dot(
-                w1t[:, width:], gear[s, :, lane(r, 2)].astype(BF), preferred_element_type=F32
-            )
-        for x in range(xrows):
-            outer[s, x] = pulled_row(0, x).astype(BF)
-        for item in returns(s):
-            start(item)
+            dhid[s, :, lane(r + 2, 2)] = pulled.astype(BF)
+            gcur[s, :, lane(r + 2, 2)] = (lag[0] + lag[1] + lag[2]).astype(BF)
+
+        for t in range(count - 1):
+            @pl.when(s == t)
+            def _():
+                borrowed(t)
+                if t == count - 2:
+                    borrowed(t + 1)
         return 0
 
+    for item in ahead[2:4]:
+        arrive(item)
     lax.fori_loop(0, count, section, 0)
 
-    def chunk(t, r):
-        gcur[t, width:, lane(r, 2)] = gear[t + count, :, lane(r, 2)].astype(BF)
-        mix[t, :, lane(r, 2)] = jnp.dot(w1t[...], gcur[t, :, lane(r, 2)], preferred_element_type=F32)
-
-    def own_edge(t, _):
-        chunk(t, 0)
-        chunk(t, hrows - 2)
+    own_halves = []
+    for t in range(count):
+        halves = [(wcur, lambda at, t=t: gcur[t, :, at])]
+        view = earlier(t + count)
+        own_halves.append(halves if view is None else halves + [(wear, view)])
+    for t in range(count):
         for i in range(2):
-            for r in range(2):
-                rims[i, t, r] = pulled_row(t, r + i * (xrows - 2)).astype(BF)
+            for r, value in enumerate(pulled_rows(i * (xrows - 2), own_halves[t])):
+                rims[i, t, r] = value.astype(BF)
         for item in edges(t):
             start(item)
-        return 0
-
-    def own_inner(t, _):
-        for r in range(2, hrows - 2, 2):
-            chunk(t, r)
-        for x in range(2, 2 + rows):
-            grad[t, x - 2] = pulled_row(t, x)
-        return 0
-
-    lax.fori_loop(0, count, own_edge, 0)
-    lax.fori_loop(0, count, own_inner, 0)
+    for t in range(count):
+        for x in range(2, 2 + rows, 2):
+            for r, value in enumerate(pulled_rows(x, own_halves[t])):
+                grad[t, x - 2 + r] = value
 
     for i, (source, ds, dt) in enumerate(((back, -1, 0), (fold, -1, -1), (fold, -1, 1), (fold, 0, -1), (fold, 0, 1))):
         @pl.when(jnp.logical_not(exists(-ds, -dt)))
@@ -295,19 +347,6 @@
         leave(item)
 
 
-def weights_of(first_kernel, first_bias, second_kernel):
-    width, chans = first_kernel.shape[2], first_kernel.shape[3] // 2
-    split = first_kernel.reshape(3, 3, width, 2, chans)
-    w1 = split.transpose(3, 2, 0, 1, 4).reshape(2 * width, 9 * chans)
-    w1t = split.transpose(1, 0, 4, 3, 2).reshape(9 * chans, 2 * width)
-    taps = second_kernel.transpose(1, 0, 2, 3).reshape(9, 1, 2, 1, width)
-    eye = jnp.eye(LAGS, dtype=BF).reshape(1, LAGS, 1, LAGS, 1)
-    w2 = (taps * eye).reshape(9, 2 * LAGS, LAGS * width)
-    w2 = jnp.pad(w2, ((0, 1), (0, 8 - 2 * LAGS), (0, 0))).reshape(80, LAGS * width)
-    b1 = jnp.broadcast_to(first_bias[:, None], (width, 128))
-    return w1, w1t, b1, w2, w2.T
-
-
 def body(
     features, vote_grad, sharpness, valid_rows, first_kernel, first_bias, second_kernel, second_bias
 ):
@@ -316,7 +355,6 @@
     hrows, xrows = rows + 2, rows + 4
 
     own = features.transpose(0, 2, 1, 3)
-    w1, w1t, b1, w2, w2t = weights_of(first_kernel, first_bias, second_kernel)
 
     vmem = pl.BlockSpec(memory_space=pltpu.VMEM)
     smem = pl.BlockSpec(memory_space=pltpu.SMEM)
@@ -326,9 +364,20 @@
             jax.ShapeDtypeStruct((count, 2, rows, cols), F32),
             jax.ShapeDtypeStruct((count, rows, chans, cols), F32),
         ),
-        in_specs=[vmem] * 2 + [smem] * 2 + [vmem] * 5 + [smem],
+        in_specs=[vmem] + [smem] * 3 + [pl.BlockSpec(memory_space=pl.ANY)] * 4,
         out_specs=(vmem, vmem),
         scratch_shapes=[
+            pltpu.VMEM(vote_grad.shape, F32),
+            pltpu.VMEM(first_kernel.shape, BF),
+            pltpu.VMEM(second_kernel.shape, BF),
+            pltpu.VMEM((1, width), F32),
+            pltpu.VMEM((2 * width, 9 * chans), BF),
+            pltpu.VMEM((3 * chans, 3 * width), BF),
+            pltpu.VMEM((3 * chans, 3 * width), BF),
+            pltpu.VMEM((width, 128), F32),
+            pltpu.VMEM((128, 256), F32),
+            pltpu.VMEM((80, LAGS * width), BF),
+            pltpu.VMEM((LAGS * width, 80), BF),
             pltpu.VMEM((count, rows, chans, cols), BF),
             pltpu.VMEM((2 * count, 2, chans, cols), BF),
             pltpu.VMEM((2 * count, 2, chans, cols), BF),
@@ -339,23 +388,27 @@
             pltpu.VMEM((rows, 8, cols), F32),
             pltpu.VMEM((xrows, 8, cols), F32),
             pltpu.VMEM((80, hrows * cols), BF),
-            pltpu.VMEM((count, 2 * width, hrows * cols), BF),
-            pltpu.VMEM((2 * count, width, hrows * cols), F32),
-            pltpu.VMEM((count, 9 * chans, hrows * cols), F32),
+            pltpu.VMEM((count, LAGS * width, (hrows + 4) * cols), BF),
+            pltpu.VMEM((count, width, (hrows + 4) * cols), BF),
+            pltpu.VMEM((2 * count, width, (hrows + 4) * cols), BF),
             pltpu.VMEM((count, xrows, chans, cols), BF),
             pltpu.VMEM((2, count, 2, chans, cols), BF),
             pltpu.VMEM((count, rows, chans, cols), BF),
             pltpu.VMEM((2, 2 * count, 2, chans, cols), BF),
-            pltpu.SemaphoreType.DMA((5,)),
-            pltpu.SemaphoreType.DMA((5,)),
+            pltpu.SemaphoreType.DMA((4 + count,)),
+            pltpu.SemaphoreType.DMA((4 + count,)),
             pltpu.SemaphoreType.DMA((5, count)),
             pltpu.SemaphoreType.DMA((5, count)),
+            pltpu.SemaphoreType.DMA((4,)),
         ],
         compiler_params=pltpu.CompilerParams(
             vmem_limit_bytes=48 * 1024 * 1024, collective_id=0, has_side_effects=True
         ),
         cost_estimate=pl.CostEstimate(flops=3 * 10**9, bytes_accessed=6 * 10**6, transcendentals=0),
-    )(own, vote_grad, sharpness, valid_rows, w1, w1t, b1, w2, w2t, second_bias)
+    )(
+        own, sharpness, valid_rows, second_bias,
+        vote_grad, first_kernel, second_kernel, first_bias.reshape(1, width),
+    )
     return voted, grad.transpose(0, 2, 1, 3)
 
 

time: 30.2 us -> 26.9 us (0.89)
  local copies, waits for them, and re-layouts: 6.48 us -> 3.77 us
  Pallas kernels: 22.7 us -> 22.3 us
    unnamed x18 -> x17, local copies, waits for them, and re-layouts: 4.73 us -> 3.77 us
    transpose x3 -> x0, local copies, waits for them, and re-layouts: 0.94 us -> none  [the longest x1 0.7 us: weights_of(): taps = second_kernel.transpose(1, 0, 2, 3).reshape(9, 1, 2, 1, width)]
    reshape x5 -> x0, local copies, waits for them, and re-layouts: 0.47 us -> none  [the longest x2 0.24 us: weights_of(): w1 = split.transpose(3, 2, 0, 1, 4).reshape(2 * width, 9 * chans)]
    pallas_call x1, Pallas kernels: 22.7 us -> 22.3 us  [body(): pl.pallas_call(kernel, out_shape=(jax.ShapeDtypeStruct((count, 2, rows, c...]
where the time goes in v2:
time: 26.9 us; the launch traced here: 26.8 us
  Pallas kernels  22.3 us (83%)
  local copies, waits for them, and re-layouts  3.77 us (14%)
  between operations  0.73 us (3%)
    pallas_call x1, Pallas kernels, body(): pl.pallas_call(kernel, out_shape=(jax.ShapeDtypeStruct((count, 2, rows, c...  22.3 us
    unnamed x17, local copies, waits for them, and re-layouts  3.77 us

profile of v2, /device:TPU:11, one launch (start us, length us, event | category | flops | bytes accessed | tf_op | source)
XLA Modules:
  0.0 26.8 jit_solution(12012050889332081735)
XLA Ops:
  0.6 0.0 copy-start
  0.6 0.0 copy-start.1
  0.7 0.0 copy-start.2
  0.7 0.0 copy-start.6
  0.7 1.2 %copy.13 = bf16[3,32,16,128]{3,1,2,0:T(8,128)(2,1)S(1)} copy(bf16[3,32,16,128]{3,2,1,0:T(8,128)(2,1)} %param.8) | data formatting | bytes 786432 | tf_op args[0]
  1.8 0.0 copy-start.3
  1.9 0.0 copy-start.4
  1.9 0.0 copy-start.5
  1.9 0.0 copy-done
  1.9 0.0 copy-done.1
  1.9 0.0 copy-done.2
  1.9 0.0 copy-done.6
  1.9 0.6 %copy-done.3 = f32[3]{0:T(128)S(1)} copy-done((f32[3]{0:T(128)S(1)}, f32[3]{0:T(128)}, u32[]{:S(2)}) %copy-start.3) | copy-done | bytes 36
  2.5 0.0 copy-done.4
  2.5 0.0 copy-done.5
  2.5 22.3 %shard_map.95 = (f32[3,2,16,128]{3,2,1,0:T(8,128)S(1)}, f32[3,16,32,128]{3,2,1,0:T(8,128)S(1)}) custom-call(bf16[3,16,32,128]{3,2,1,0:T(8,128)(2,1)S(1)} %bitcast.6, f32[3]{0:T(128)S(1)} %copy-done.3, s32[3]{0:T(128)S(1)} %copy-done.4, f32[2]{0:T(128)S(1)} %copy-done.5, f32[3,2,16,128]{3,2,1,0:T(8,128)S(1)} %copy-done.1, bf16[3,3,64,64]{3,2,1,0:T(8,128)(2,1)S(1)} %copy-done, ...), custom_call_target="tpu_custom_call" | custom-call | flops 3000000000 | bytes 6000000 | tf_op jit(solution)/shard_map/pallas_call | solution.py:361
  24.8 1.3 %copy.11 = f32[3,32,16,128]{3,2,1,0:T(8,128)} copy(f32[3,32,16,128]{3,1,2,0:T(8,128)S(1)} %bitcast.5) | data formatting | bytes 1572864
  26.2 0.6 %copy.15 = f32[3,2,16,128]{3,2,1,0:T(8,128)} copy(f32[3,2,16,128]{3,2,1,0:T(8,128)S(1)} %get-tuple-element.10) | data formatting | bytes 98304
Async XLA Ops:
  0.6 1.2 %copy-start = (bf16[3,3,64,64]{3,2,1,0:T(8,128)(2,1)S(1)}, bf16[3,3,64,64]{3,2,1,0:T(8,128)(2,1)}, u32[]{:S(2)}) copy-start(bf16[3,3,64,64]{3,2,1,0:T(8,128)(2,1)} %fk_hbm.1) | copy-start | bytes 221188
  0.6 1.2 %copy-start.1 = (f32[3,2,16,128]{3,2,1,0:T(8,128)S(1)}, f32[3,2,16,128]{3,2,1,0:T(8,128)}, u32[]{:S(2)}) copy-start(f32[3,2,16,128]{3,2,1,0:T(8,128)} %cot_hbm.1) | copy-start | bytes 147460
  0.7 1.2 %copy-start.2 = (bf16[3,3,2,64]{3,2,1,0:T(2,128)(2,1)S(1)}, bf16[3,3,2,64]{3,2,1,0:T(2,128)(2,1)}, u32[]{:S(2)}) copy-start(bf16[3,3,2,64]{3,2,1,0:T(2,128)(2,1)} %sk_hbm.1) | copy-start | bytes 6916
  0.7 1.2 %copy-start.6 = (f32[64]{0:T(128)S(1)}, f32[64]{0:T(128)}, u32[]{:S(2)}) copy-start(f32[64]{0:T(128)} %param.13) | copy-start | bytes 772
  1.8 0.7 %copy-start.3 = (f32[3]{0:T(128)S(1)}, f32[3]{0:T(128)}, u32[]{:S(2)}) copy-start(f32[3]{0:T(128)} %sharp.1) | copy-start | bytes 40
  1.9 0.7 %copy-start.4 = (s32[3]{0:T(128)S(1)}, s32[3]{0:T(128)}, u32[]{:S(2)}) copy-start(s32[3]{0:T(128)} %valid.1) | copy-start | bytes 40
  1.9 0.7 %copy-start.5 = (f32[2]{0:T(128)S(1)}, f32[2]{0:T(128)}, u32[]{:S(2)}) copy-start(f32[2]{0:T(128)} %b2.1) | copy-start | bytes 28

commit v3 on v2

--- a/solution.py
+++ b/solution.py
@@ -120,6 +120,11 @@
         def _():
             to[...] = jnp.zeros(to.shape, BF)
 
+    near = lambda low, high: low.astype(jnp.int32) + high.astype(jnp.int32) + 1
+    pl.semaphore_wait(barrier, near(sec > 0, sec < secs - 1) * near(tile > 0, tile < tiles - 1) - 1)
+    for item in ahead:
+        start(item)
+
     for ref in (dhid, gcur, gear):
         for row in (0, hrows + 2):
             ref[:, :, lane(row, 2)] = jnp.zeros(ref.shape[:2] + (2 * cols,), BF)
@@ -133,11 +138,6 @@
         at = slice(half * chans, (half + 1) * chans)
         taps = [wide[dy][dx][:, at] for dy in range(3) for dx in range(3)]
         w1[half * width:(half + 1) * width, :] = jnp.concatenate(taps, axis=1).astype(BF)
-
-    near = lambda low, high: low.astype(jnp.int32) + high.astype(jnp.int32) + 1
-    pl.semaphore_wait(barrier, near(sec > 0, sec < secs - 1) * near(tile > 0, tile < tiles - 1) - 1)
-    for item in ahead:
-        start(item)
 
     for dx in range(3):
         turned = [wide[dy][dx].T for dy in range(3)]

time: 26.9 us -> 27 us (level)
  no operation moved by 1% of the time
where the time goes in v3:
time: 27 us; the launch traced here: 26.8 us
  Pallas kernels  22.3 us (83%)
  local copies, waits for them, and re-layouts  3.77 us (14%)
  between operations  0.73 us (3%)
    pallas_call x1, Pallas kernels, body(): pl.pallas_call(kernel, out_shape=(jax.ShapeDtypeStruct((count, 2, rows, c...  22.3 us
    unnamed x17, local copies, waits for them, and re-layouts  3.77 us

profile of v3, /device:TPU:11, one launch (start us, length us, event | category | flops | bytes accessed | tf_op | source)
XLA Modules:
  0.0 26.8 jit_solution(5209620330398877960)
XLA Ops:
  0.6 0.0 copy-start
  0.6 0.0 copy-start.1
  0.7 0.0 copy-start.2
  0.7 0.0 copy-start.6
  0.7 1.2 %copy.13 = bf16[3,32,16,128]{3,1,2,0:T(8,128)(2,1)S(1)} copy(bf16[3,32,16,128]{3,2,1,0:T(8,128)(2,1)} %param.8) | data formatting | bytes 786432 | tf_op args[0]
  1.8 0.0 copy-start.3
  1.9 0.0 copy-start.4
  1.9 0.0 copy-start.5
  1.9 0.0 copy-done
  1.9 0.0 copy-done.1
  1.9 0.0 copy-done.2
  1.9 0.0 copy-done.6
  1.9 0.6 %copy-done.3 = f32[3]{0:T(128)S(1)} copy-done((f32[3]{0:T(128)S(1)}, f32[3]{0:T(128)}, u32[]{:S(2)}) %copy-start.3) | copy-done | bytes 36
  2.5 0.0 copy-done.4
  2.5 0.0 copy-done.5
  2.5 22.3 %shard_map.95 = (f32[3,2,16,128]{3,2,1,0:T(8,128)S(1)}, f32[3,16,32,128]{3,2,1,0:T(8,128)S(1)}) custom-call(bf16[3,16,32,128]{3,2,1,0:T(8,128)(2,1)S(1)} %bitcast.6, f32[3]{0:T(128)S(1)} %copy-done.3, s32[3]{0:T(128)S(1)} %copy-done.4, f32[2]{0:T(128)S(1)} %copy-done.5, f32[3,2,16,128]{3,2,1,0:T(8,128)S(1)} %copy-done.1, bf16[3,3,64,64]{3,2,1,0:T(8,128)(2,1)S(1)} %copy-done, ...), custom_call_target="tpu_custom_call" | custom-call | flops 3000000000 | bytes 6000000 | tf_op jit(solution)/shard_map/pallas_call | solution.py:361
  24.8 1.3 %copy.11 = f32[3,32,16,128]{3,2,1,0:T(8,128)} copy(f32[3,32,16,128]{3,1,2,0:T(8,128)S(1)} %bitcast.5) | data formatting | bytes 1572864
  26.2 0.6 %copy.15 = f32[3,2,16,128]{3,2,1,0:T(8,128)} copy(f32[3,2,16,128]{3,2,1,0:T(8,128)S(1)} %get-tuple-element.10) | data formatting | bytes 98304
Async XLA Ops:
  0.6 1.2 %copy-start = (bf16[3,3,64,64]{3,2,1,0:T(8,128)(2,1)S(1)}, bf16[3,3,64,64]{3,2,1,0:T(8,128)(2,1)}, u32[]{:S(2)}) copy-start(bf16[3,3,64,64]{3,2,1,0:T(8,128)(2,1)} %fk_hbm.1) | copy-start | bytes 221188
  0.6 1.2 %copy-start.1 = (f32[3,2,16,128]{3,2,1,0:T(8,128)S(1)}, f32[3,2,16,128]{3,2,1,0:T(8,128)}, u32[]{:S(2)}) copy-start(f32[3,2,16,128]{3,2,1,0:T(8,128)} %cot_hbm.1) | copy-start | bytes 147460
  0.7 1.2 %copy-start.2 = (bf16[3,3,2,64]{3,2,1,0:T(2,128)(2,1)S(1)}, bf16[3,3,2,64]{3,2,1,0:T(2,128)(2,1)}, u32[]{:S(2)}) copy-start(bf16[3,3,2,64]{3,2,1,0:T(2,128)(2,1)} %sk_hbm.1) | copy-start | bytes 6916
  0.7 1.2 %copy-start.6 = (f32[64]{0:T(128)S(1)}, f32[64]{0:T(128)}, u32[]{:S(2)}) copy-start(f32[64]{0:T(128)} %param.13) | copy-start | bytes 772
  1.8 0.7 %copy-start.3 = (f32[3]{0:T(128)S(1)}, f32[3]{0:T(128)}, u32[]{:S(2)}) copy-start(f32[3]{0:T(128)} %sharp.1) | copy-start | bytes 40
  1.9 0.7 %copy-start.4 = (s32[3]{0:T(128)S(1)}, s32[3]{0:T(128)}, u32[]{:S(2)}) copy-start(s32[3]{0:T(128)} %valid.1) | copy-start | bytes 40
  1.9 0.7 %copy-start.5 = (f32[2]{0:T(128)S(1)}, f32[2]{0:T(128)}, u32[]{:S(2)}) copy-start(f32[2]{0:T(128)} %b2.1) | copy-start | bytes 28

commit v4 on v3

--- a/solution.py
+++ b/solution.py
@@ -20,9 +20,9 @@
 
 
 def kernel(
-    own, sharp, valid, b2, cot_hbm, fk_hbm, sk_hbm, b1_hbm,
+    feat, sharp, valid, b2, cot_hbm, fk_hbm, sk_hbm, b1_hbm,
     voted, grad,
-    cot, fk, sk, bias, w1, wcur, wear, b1, w2f, w2, w2t,
+    stage, own, cot, fk, sk, bias, w1, wcur, wear, b1, w2f, w2, w2t,
     prev, top, bot, xs, ab, hid, tap, fld, dfl, dst, dhid, gcur, gear,
     outer, rims, back, fold,
     fsend, frecv, bsend, brecv, local,
@@ -119,6 +119,11 @@
         @pl.when(jnp.logical_not(exists(-ds, -dt)))
         def _():
             to[...] = jnp.zeros(to.shape, BF)
+
+    stage[...] = feat[...].astype(F32)
+    for t in range(count):
+        for r in range(rows):
+            own[t, r] = stage[t, pl.ds(r, chans, stride=rows), :].astype(BF)
 
     near = lambda low, high: low.astype(jnp.int32) + high.astype(jnp.int32) + 1
     pl.semaphore_wait(barrier, near(sec > 0, sec < secs - 1) * near(tile > 0, tile < tiles - 1) - 1)
@@ -354,7 +359,7 @@
     width = first_kernel.shape[2]
     hrows, xrows = rows + 2, rows + 4
 
-    own = features.transpose(0, 2, 1, 3)
+    own = features.reshape(count, chans * rows, cols)
 
     vmem = pl.BlockSpec(memory_space=pltpu.VMEM)
     smem = pl.BlockSpec(memory_space=pltpu.SMEM)
@@ -367,6 +372,8 @@
         in_specs=[vmem] + [smem] * 3 + [pl.BlockSpec(memory_space=pl.ANY)] * 4,
         out_specs=(vmem, vmem),
         scratch_shapes=[
+            pltpu.VMEM((count, chans * rows, cols), F32),
+            pltpu.VMEM((count, rows, chans, cols), BF),
             pltpu.VMEM(vote_grad.shape, F32),
             pltpu.VMEM(first_kernel.shape, BF),
             pltpu.VMEM(second_kernel.shape, BF),

time: 27 us -> 29.3 us (1.085)
  local copies, waits for them, and re-layouts: 3.77 us -> 6.02 us
    unnamed x17 -> x18, local copies, waits for them, and re-layouts: 3.77 us -> 6.02 us
where the time goes in v4:
time: 29.3 us; the launch traced here: 29 us
  Pallas kernels  22.3 us (76%)
  local copies, waits for them, and re-layouts  6.02 us (21%)
  between operations  0.68 us (2%)
    pallas_call x1, Pallas kernels, body(): pl.pallas_call(kernel, out_shape=(jax.ShapeDtypeStruct((count, 2, rows, c...  22.3 us
    unnamed x18, local copies, waits for them, and re-layouts  6.02 us

profile of v4, /device:TPU:11, one launch (start us, length us, event | category | flops | bytes accessed | tf_op | source)
XLA Modules:
  0.0 29.0 jit_solution(18258814585141086884)
XLA Ops:
  0.6 0.0 copy-start.7
  0.6 0.0 copy-start.4
  0.7 0.0 copy-start.5
  0.7 0.0 copy-start.6
  0.7 0.6 %copy-done.7 = f32[64]{0:T(128)S(1)} copy-done((f32[64]{0:T(128)S(1)}, f32[64]{0:T(128)}, u32[]{:S(2)}) %copy-start.7) | copy-done | bytes 280
  1.3 0.0 copy-done.4
  1.3 0.0 copy-done.5
  1.3 0.0 copy-done.6
  1.3 0.0 copy-start
  1.3 1.0 %copy-done = bf16[3,32,16,128]{3,2,1,0:T(8,128)(2,1)S(1)} copy-done((bf16[3,32,16,128]{3,2,1,0:T(8,128)(2,1)S(1)}, bf16[3,32,16,128]{3,2,1,0:T(8,128)(2,1)}, u32[]{:S(2)}) %copy-start) | copy-done | bytes 393240
  2.3 0.0 copy-start.1
  2.3 0.9 %copy-done.1 = bf16[3,3,64,64]{3,2,1,0:T(8,128)(2,1)S(1)} copy-done((bf16[3,3,64,64]{3,2,1,0:T(8,128)(2,1)S(1)}, bf16[3,3,64,64]{3,2,1,0:T(8,128)(2,1)}, u32[]{:S(2)}) %copy-start.1) | copy-done | bytes 73752
  3.2 0.0 copy-start.2
  3.2 0.8 %copy-done.2 = f32[3,2,16,128]{3,2,1,0:T(8,128)S(1)} copy-done((f32[3,2,16,128]{3,2,1,0:T(8,128)S(1)}, f32[3,2,16,128]{3,2,1,0:T(8,128)}, u32[]{:S(2)}) %copy-start.2) | copy-done | bytes 49176
  4.0 0.0 copy-start.3
  4.0 0.7 %copy-done.3 = bf16[3,3,2,64]{3,2,1,0:T(2,128)(2,1)S(1)} copy-done((bf16[3,3,2,64]{3,2,1,0:T(2,128)(2,1)S(1)}, bf16[3,3,2,64]{3,2,1,0:T(2,128)(2,1)}, u32[]{:S(2)}) %copy-start.3) | copy-done | bytes 2328
  4.7 22.3 %shard_map.95 = (f32[3,2,16,128]{3,2,1,0:T(8,128)S(1)}, f32[3,16,32,128]{3,2,1,0:T(8,128)S(1)}) custom-call(bf16[3,512,128]{2,1,0:T(8,128)(2,1)S(1)} %bitcast.4, f32[3]{0:T(128)S(1)} %copy-done.4, s32[3]{0:T(128)S(1)} %copy-done.5, f32[2]{0:T(128)S(1)} %copy-done.6, f32[3,2,16,128]{3,2,1,0:T(8,128)S(1)} %copy-done.2, bf16[3,3,64,64]{3,2,1,0:T(8,128)(2,1)S(1)} %copy-done.1, ...), custom_call_target="tpu_custom_call" | custom-call | flops 3000000000 | bytes 6000000 | tf_op jit(solution)/shard_map/pallas_call | solution.py:366
  27.0 1.3 %copy.10 = f32[3,32,16,128]{3,2,1,0:T(8,128)} copy(f32[3,32,16,128]{3,1,2,0:T(8,128)S(1)} %bitcast.3) | data formatting | bytes 1572864
  28.4 0.6 %copy.12 = f32[3,2,16,128]{3,2,1,0:T(8,128)} copy(f32[3,2,16,128]{3,2,1,0:T(8,128)S(1)} %get-tuple-element.10) | data formatting | bytes 98304
Async XLA Ops:
  0.6 0.7 %copy-start.7 = (f32[64]{0:T(128)S(1)}, f32[64]{0:T(128)}, u32[]{:S(2)}) copy-start(f32[64]{0:T(128)} %param.13) | copy-start | bytes 772
  0.6 0.7 %copy-start.4 = (f32[3]{0:T(128)S(1)}, f32[3]{0:T(128)}, u32[]{:S(2)}) copy-start(f32[3]{0:T(128)} %sharp.1) | copy-start | bytes 40
  0.7 0.7 %copy-start.5 = (s32[3]{0:T(128)S(1)}, s32[3]{0:T(128)}, u32[]{:S(2)}) copy-start(s32[3]{0:T(128)} %valid.1) | copy-start | bytes 40
  0.7 0.7 %copy-start.6 = (f32[2]{0:T(128)S(1)}, f32[2]{0:T(128)}, u32[]{:S(2)}) copy-start(f32[2]{0:T(128)} %b2.1) | copy-start | bytes 28
  1.3 1.0 %copy-start = (bf16[3,32,16,128]{3,2,1,0:T(8,128)(2,1)S(1)}, bf16[3,32,16,128]{3,2,1,0:T(8,128)(2,1)}, u32[]{:S(2)}) copy-start(bf16[3,32,16,128]{3,2,1,0:T(8,128)(2,1)} %param.8) | copy-start | bytes 1179652
  2.3 0.9 %copy-start.1 = (bf16[3,3,64,64]{3,2,1,0:T(8,128)(2,1)S(1)}, bf16[3,3,64,64]{3,2,1,0:T(8,128)(2,1)}, u32[]{:S(2)}) copy-start(bf16[3,3,64,64]{3,2,1,0:T(8,128)(2,1)} %fk_hbm.1) | copy-start | bytes 221188
  3.2 0.8 %copy-start.2 = (f32[3,2,16,128]{3,2,1,0:T(8,128)S(1)}, f32[3,2,16,128]{3,2,1,0:T(8,128)}, u32[]{:S(2)}) copy-start(f32[3,2,16,128]{3,2,1,0:T(8,128)} %cot_hbm.1) | copy-start | bytes 147460
  4.0 0.7 %copy-start.3 = (bf16[3,3,2,64]{3,2,1,0:T(2,128)(2,1)S(1)}, bf16[3,3,2,64]{3,2,1,0:T(2,128)(2,1)}, u32[]{:S(2)}) copy-start(bf16[3,3,2,64]{3,2,1,0:T(2,128)(2,1)} %sk_hbm.1) | copy-start | bytes 6916
